TPU v7x, 32 devices: a whole 2x2x4 slice. The times are simulated.
32 devices in a mesh: ctx: 8 (over y, x, core), tp: 4 (over z).
Axes of the slice: x: 2, y: 2, z: 4, core: 2. Of those that a mesh axis runs over, the one named last changes fastest.
Arguments:
- queries: bfloat16 [1024, 128, 128], P('ctx', 'tp'), may hold values from -8 to 8
- fresh_rotated_keys: bfloat16 [1024, 8, 128], P('ctx', 'tp'), may hold values from -4 to 4
- fresh_value_rows: bfloat16 [1024, 8, 128], P('ctx', 'tp'), may hold values from -5 to 5
- cache_keys: bfloat16 [8192, 8, 128], P('ctx', 'tp'), may hold values from -4 to 4
- prefix_value_rows: bfloat16 [8192, 8, 128], P('ctx', 'tp'), may hold values from -5 to 5
- cache_lengths: int32 [8], P('ctx'), may hold values from 256 to 1024, as said below
- new_segment: int32 [1024], replicated, may hold values from 0 to 3, never falling along the last dimension, each value on 1 to 512 neighbouring positions
- out_weight: bfloat16 [16384, 16384], P('tp', 'ctx'), may hold values from -0.1875 to 0.1875
Outputs:
- attended: bfloat16 [1024, 128, 128], P('ctx', 'tp')
- mixed: bfloat16 [1024, 16384], P('tp', 'ctx')
Inputs may be any that keep to these rules, and one draw needn't show every extreme that they name: `cache_lengths`: slots at or after the length of their index are unused; some index is full in every draw.
All inputs are finite; a program needn't handle non-finite values.
Results may differ from a plain program's by a relative error of at most 0.015.
Values may be sent and summed in bfloat16 or wider, within the bound.
A program may use at most 128 MiB of HBM per device.

v0:
```python
import jax
import jax.numpy as jnp
from jax import lax
from jax.sharding import PartitionSpec as P

lowest_score_bound = -1e30


def attend(query_block, key_rows, value_rows, visible, scaling):
    scores = (
        jnp.einsum("qhrd,khd->hqrk", query_block, key_rows, preferred_element_type=jnp.float32)
        * scaling
    )
    scores = jnp.where(visible[None, :, None, :], scores, lowest_score_bound)
    highest = jnp.max(scores, axis=-1)
    weights = jnp.exp(scores - highest[..., None])
    total = jnp.sum(weights, axis=-1)
    mixture = jnp.einsum(
        "hqrk,khd->qhrd",
        weights.astype(jnp.bfloat16),
        value_rows,
        preferred_element_type=jnp.float32,
    )
    mixture = mixture / jnp.transpose(total, (1, 0, 2))[..., None]
    log_mass = jnp.transpose(highest + jnp.log(total), (1, 0, 2))
    return (mixture.astype(jnp.bfloat16), log_mass)


def visibility(query_start, rows, shard, length, new_segment, cache_rows):
    query_pos = query_start + jnp.arange(rows, dtype=jnp.int32)
    key_start = shard * rows
    key_pos = key_start + jnp.arange(rows, dtype=jnp.int32)
    query_seg = lax.dynamic_slice_in_dim(new_segment, query_start, rows, 0)
    key_seg = lax.dynamic_slice_in_dim(new_segment, key_start, rows, 0)
    cache_ok = jnp.broadcast_to(
        (jnp.arange(cache_rows, dtype=jnp.int32) < length)[None, :], (rows, cache_rows)
    )
    new_ok = (query_seg[:, None] == key_seg[None, :]) & (key_pos[None, :] <= query_pos[:, None])
    return jnp.concatenate([cache_ok, new_ok], 1)


def combine(state, mixture, log_mass):
    run_max, run_sum, accum = state
    highest = jnp.maximum(run_max, log_mass)
    kept = jnp.exp(run_max - highest)
    fresh = jnp.exp(log_mass - highest)
    return (
        highest,
        run_sum * kept + fresh,
        accum * kept[..., None] + fresh[..., None] * mixture.astype(jnp.float32),
    )


def on_device(
    queries,
    fresh_rotated_keys,
    fresh_value_rows,
    cache_keys,
    prefix_value_rows,
    cache_lengths,
    new_segment,
    out_weight,
):
    rows, heads, width = queries.shape
    kv_heads = fresh_rotated_keys.shape[1]
    query_group = heads // kv_heads
    cache_rows = cache_keys.shape[0]
    here = lax.axis_index("ctx")
    scaling = width ** (-0.5)
    local_keys = jnp.concatenate([cache_keys, fresh_rotated_keys], 0)
    local_values = jnp.concatenate([prefix_value_rows, fresh_value_rows], 0)
    all_lengths = lax.all_gather(cache_lengths, "ctx", axis=0, tiled=True)
    own_block = queries.reshape(rows, kv_heads, query_group, width)
    piece_rows = cache_rows + rows
    initial_state = (
        jnp.full((rows, kv_heads, query_group), lowest_score_bound, jnp.float32),
        jnp.zeros((rows, kv_heads, query_group), jnp.float32),
        jnp.zeros((rows, kv_heads, query_group, width), jnp.float32),
    )
    state = initial_state
    key_piece = lax.all_gather(local_keys, "ctx", axis=0, tiled=True)
    value_piece = lax.all_gather(local_values, "ctx", axis=0, tiled=True)
    count = key_piece.shape[0] // piece_rows
    key_stack = key_piece.reshape(count, piece_rows, kv_heads, width)
    value_stack = value_piece.reshape(count, piece_rows, kv_heads, width)

    def step(inner, inputs):
        key_rows, value_rows, offset = inputs
        length = lax.dynamic_slice_in_dim(all_lengths, offset, 1, 0)[0]
        visible = visibility(here * rows, rows, offset, length, new_segment, cache_rows)
        mixture, log_mass = attend(own_block, key_rows, value_rows, visible, scaling)
        return (combine(inner, mixture, log_mass), None)

    state, _ = lax.scan(step, state, (key_stack, value_stack, jnp.arange(count, dtype=jnp.int32)))
    run_max, run_sum, accum = state
    merged = accum / run_sum[..., None]
    attended = merged.astype(jnp.bfloat16).reshape(rows, heads, width)
    flat = attended.reshape(rows, heads * width)
    partial_sums = jnp.dot(
        lax.all_gather(flat, "ctx", axis=0, tiled=True),
        out_weight,
        preferred_element_type=jnp.float32,
    )
    mixed = lax.psum_scatter(partial_sums, "tp", scatter_dimension=0, tiled=True).astype(
        jnp.bfloat16
    )
    return (attended, mixed)


def solution(mesh):
    in_specs = (
        P("ctx", "tp", None),
        P("ctx", "tp", None),
        P("ctx", "tp", None),
        P("ctx", "tp", None),
        P("ctx", "tp", None),
        P("ctx"),
        P(),
        P("tp", "ctx"),
    )
    out_specs = (P("ctx", "tp", None), P("tp", "ctx"))
    return jax.shard_map(
        on_device, mesh=mesh, in_specs=in_specs, out_specs=out_specs, check_vma=False
    )
```

profile of v0, /device:TPU:0, one launch (start us, length us, event | category | flops | bytes accessed | tf_op | source)
XLA Modules:
  0.0 585.4 jit_solution(1085600874858464554)
XLA Ops:
  15.2 9.5 %all-reduce = s32[8]{0:T(128)S(1)} all-reduce(s32[8]{0:T(128)S(1)} %dynamic-update-slice), channel_id=1, replica_groups=mesh['ctx'=8,'tp'=4] {'ctx'}, use_global_device_ids=true, to_apply=%add | all-reduce | flops 8 | bytes 64
  27.0 25.2 %all-gather.4.cloned.1.call-done = bf16[9216,2,128]{2,0,1:T(8,128)(2,1)} async-done(((bf16[1152,2,128]{2,0,1:T(8,128)(2,1)}), bf16[9216,2,128]{2,0,1:T(8,128)(2,1)}) %all-gather.4.cloned.1.call-update) | async-done | bytes 4718608 | tf_op jit(solution)/shard_map/all_gather | solution.py:81
  52.2 41.4 %all-gather.6.cloned.1.call-done = bf16[9216,2,128]{2,0,1:T(8,128)(2,1)} async-done(((bf16[1152,2,128]{2,0,1:T(8,128)(2,1)}), bf16[9216,2,128]{2,0,1:T(8,128)(2,1)}) %all-gather.6.cloned.1.call-update) | async-done | bytes 4718608 | tf_op jit(solution)/shard_map/all_gather | solution.py:82
  93.6 256.3 %while.17 = (s32[]{:T(128)}, f32[128,2,16]{0,2,1:T(8,128)S(1)}, f32[128,2,16]{0,2,1:T(8,128)S(1)}, f32[128,2,16,128]{0,3,2,1:T(8,128)S(1)}, s32[8]{0:T(128)S(1)}...) while((s32[]{:T(128)}, f32[128,2,16]{0,2,1:T(8,128)S(1)}, ...), condition=%wide.region_3.4_spmd.clone, body=%wide.region_0.3_spmd.clone.sunk | while | flops 2452841728 | bytes 63628840 | solution.py:94
  99.2 8.9 %fusion.33 = (f32[2,128,16]{1,2,0:T(8,128)S(1)}, f32[2,128,16,1152]{1,3,2,0:T(8,128)}) fusion(bf16[128,2,16,128]{3,0,2,1:T(8,128)(2,1)S(1)} %get-tuple-element.359, bf16[8,1152,2,128]{3,1,0,2:T(8,128)(2,1)} %get-tuple-element.358, s32[]{:T(128)} %get-tuple-element.331, pred[128,1152]{0,1:T(8,128)(4,1)S(1)} %pad_add_fusion.2), kind=kOutput, calls=%fused_computation.30.clone.1 | convolution fusion | flops 1222111232 | bytes 20677120 | tf_op jit(solution)/shard_map/while/body/eval_jaxpr/qhrd,khd->hqrk/dot_general | solution.py:11
  108.0 9.2 %fusion.34 = f32[2,128,16]{1,2,0:T(8,128)S(1)} fusion(f32[2,128,16,1152]{1,3,2,0:T(8,128)} %get-tuple-element.307, f32[2,128,16]{1,2,0:T(8,128)S(1)} %get-tuple-element.308), kind=kLoop, calls=%fused_computation.3.clone.1 | loop fusion | flops 9433088 | bytes 18907136 | tf_op jit(solution)/shard_map/while/body/eval_jaxpr/reduce_sum | solution.py:17
  117.2 8.4 %fusion.36 = f32[128,2,16,128]{0,3,2,1:T(8,128)S(1)} fusion(f32[128,2,16,128]{0,3,2,1:T(8,128)S(1)} %get-tuple-element.334, f32[2,128,16,1152]{1,3,2,0:T(8,128)} %get-tuple-element.307, f32[2,128,16]{1,2,0:T(8,128)S(1)} %get-tuple-element.308, f32[128,2,16]{0,2,1:T(8,128)S(1)} %bitcast.65, f32[128,2,16]{0,2,1:T(8,128)S(1)} %get-tuple-element.311, ...), kind=kOutput, calls=%fused_computation.9.clone.1 | convolution fusion | flops 1221066752 | bytes 23724544 | tf_op jit(solution)/shard_map/while/body/eval_jaxpr/hqrk,khd->qhrd/dot_general | solution.py:18
  131.2 8.9 %fusion.33 = (f32[2,128,16]{1,2,0:T(8,128)S(1)}, f32[2,128,16,1152]{1,3,2,0:T(8,128)}) fusion(bf16[128,2,16,128]{3,0,2,1:T(8,128)(2,1)S(1)} %get-tuple-element.359, bf16[8,1152,2,128]{3,1,0,2:T(8,128)(2,1)} %get-tuple-element.358, s32[]{:T(128)} %get-tuple-element.331, pred[128,1152]{0,1:T(8,128)(4,1)S(1)} %pad_add_fusion.2), kind=kOutput, calls=%fused_computation.30.clone.1 | convolution fusion | flops 1222111232 | bytes 20677120 | tf_op jit(solution)/shard_map/while/body/eval_jaxpr/qhrd,khd->hqrk/dot_general | solution.py:11
  140.1 9.2 %fusion.34 = f32[2,128,16]{1,2,0:T(8,128)S(1)} fusion(f32[2,128,16,1152]{1,3,2,0:T(8,128)} %get-tuple-element.307, f32[2,128,16]{1,2,0:T(8,128)S(1)} %get-tuple-element.308), kind=kLoop, calls=%fused_computation.3.clone.1 | loop fusion | flops 9433088 | bytes 18907136 | tf_op jit(solution)/shard_map/while/body/eval_jaxpr/reduce_sum | solution.py:17
  149.3 8.4 %fusion.36 = f32[128,2,16,128]{0,3,2,1:T(8,128)S(1)} fusion(f32[128,2,16,128]{0,3,2,1:T(8,128)S(1)} %get-tuple-element.334, f32[2,128,16,1152]{1,3,2,0:T(8,128)} %get-tuple-element.307, f32[2,128,16]{1,2,0:T(8,128)S(1)} %get-tuple-element.308, f32[128,2,16]{0,2,1:T(8,128)S(1)} %bitcast.65, f32[128,2,16]{0,2,1:T(8,128)S(1)} %get-tuple-element.311, ...), kind=kOutput, calls=%fused_computation.9.clone.1 | convolution fusion | flops 1221066752 | bytes 23724544 | tf_op jit(solution)/shard_map/while/body/eval_jaxpr/hqrk,khd->qhrd/dot_general | solution.py:18
  163.2 8.9 %fusion.33 = (f32[2,128,16]{1,2,0:T(8,128)S(1)}, f32[2,128,16,1152]{1,3,2,0:T(8,128)}) fusion(bf16[128,2,16,128]{3,0,2,1:T(8,128)(2,1)S(1)} %get-tuple-element.359, bf16[8,1152,2,128]{3,1,0,2:T(8,128)(2,1)} %get-tuple-element.358, s32[]{:T(128)} %get-tuple-element.331, pred[128,1152]{0,1:T(8,128)(4,1)S(1)} %pad_add_fusion.2), kind=kOutput, calls=%fused_computation.30.clone.1 | convolution fusion | flops 1222111232 | bytes 20677120 | tf_op jit(solution)/shard_map/while/body/eval_jaxpr/qhrd,khd->hqrk/dot_general | solution.py:11
  172.1 9.2 %fusion.34 = f32[2,128,16]{1,2,0:T(8,128)S(1)} fusion(f32[2,128,16,1152]{1,3,2,0:T(8,128)} %get-tuple-element.307, f32[2,128,16]{1,2,0:T(8,128)S(1)} %get-tuple-element.308), kind=kLoop, calls=%fused_computation.3.clone.1 | loop fusion | flops 9433088 | bytes 18907136 | tf_op jit(solution)/shard_map/while/body/eval_jaxpr/reduce_sum | solution.py:17
  181.3 8.4 %fusion.36 = f32[128,2,16,128]{0,3,2,1:T(8,128)S(1)} fusion(f32[128,2,16,128]{0,3,2,1:T(8,128)S(1)} %get-tuple-element.334, f32[2,128,16,1152]{1,3,2,0:T(8,128)} %get-tuple-element.307, f32[2,128,16]{1,2,0:T(8,128)S(1)} %get-tuple-element.308, f32[128,2,16]{0,2,1:T(8,128)S(1)} %bitcast.65, f32[128,2,16]{0,2,1:T(8,128)S(1)} %get-tuple-element.311, ...), kind=kOutput, calls=%fused_computation.9.clone.1 | convolution fusion | flops 1221066752 | bytes 23724544 | tf_op jit(solution)/shard_map/while/body/eval_jaxpr/hqrk,khd->qhrd/dot_general | solution.py:18
  195.3 8.9 %fusion.33 = (f32[2,128,16]{1,2,0:T(8,128)S(1)}, f32[2,128,16,1152]{1,3,2,0:T(8,128)}) fusion(bf16[128,2,16,128]{3,0,2,1:T(8,128)(2,1)S(1)} %get-tuple-element.359, bf16[8,1152,2,128]{3,1,0,2:T(8,128)(2,1)} %get-tuple-element.358, s32[]{:T(128)} %get-tuple-element.331, pred[128,1152]{0,1:T(8,128)(4,1)S(1)} %pad_add_fusion.2), kind=kOutput, calls=%fused_computation.30.clone.1 | convolution fusion | flops 1222111232 | bytes 20677120 | tf_op jit(solution)/shard_map/while/body/eval_jaxpr/qhrd,khd->hqrk/dot_general | solution.py:11
  204.1 9.2 %fusion.34 = f32[2,128,16]{1,2,0:T(8,128)S(1)} fusion(f32[2,128,16,1152]{1,3,2,0:T(8,128)} %get-tuple-element.307, f32[2,128,16]{1,2,0:T(8,128)S(1)} %get-tuple-element.308), kind=kLoop, calls=%fused_computation.3.clone.1 | loop fusion | flops 9433088 | bytes 18907136 | tf_op jit(solution)/shard_map/while/body/eval_jaxpr/reduce_sum | solution.py:17
  213.3 8.4 %fusion.36 = f32[128,2,16,128]{0,3,2,1:T(8,128)S(1)} fusion(f32[128,2,16,128]{0,3,2,1:T(8,128)S(1)} %get-tuple-element.334, f32[2,128,16,1152]{1,3,2,0:T(8,128)} %get-tuple-element.307, f32[2,128,16]{1,2,0:T(8,128)S(1)} %get-tuple-element.308, f32[128,2,16]{0,2,1:T(8,128)S(1)} %bitcast.65, f32[128,2,16]{0,2,1:T(8,128)S(1)} %get-tuple-element.311, ...), kind=kOutput, calls=%fused_computation.9.clone.1 | convolution fusion | flops 1221066752 | bytes 23724544 | tf_op jit(solution)/shard_map/while/body/eval_jaxpr/hqrk,khd->qhrd/dot_general | solution.py:18
  227.3 8.9 %fusion.33 = (f32[2,128,16]{1,2,0:T(8,128)S(1)}, f32[2,128,16,1152]{1,3,2,0:T(8,128)}) fusion(bf16[128,2,16,128]{3,0,2,1:T(8,128)(2,1)S(1)} %get-tuple-element.359, bf16[8,1152,2,128]{3,1,0,2:T(8,128)(2,1)} %get-tuple-element.358, s32[]{:T(128)} %get-tuple-element.331, pred[128,1152]{0,1:T(8,128)(4,1)S(1)} %pad_add_fusion.2), kind=kOutput, calls=%fused_computation.30.clone.1 | convolution fusion | flops 1222111232 | bytes 20677120 | tf_op jit(solution)/shard_map/while/body/eval_jaxpr/qhrd,khd->hqrk/dot_general | solution.py:11
  236.2 9.2 %fusion.34 = f32[2,128,16]{1,2,0:T(8,128)S(1)} fusion(f32[2,128,16,1152]{1,3,2,0:T(8,128)} %get-tuple-element.307, f32[2,128,16]{1,2,0:T(8,128)S(1)} %get-tuple-element.308), kind=kLoop, calls=%fused_computation.3.clone.1 | loop fusion | flops 9433088 | bytes 18907136 | tf_op jit(solution)/shard_map/while/body/eval_jaxpr/reduce_sum | solution.py:17
  245.4 8.4 %fusion.36 = f32[128,2,16,128]{0,3,2,1:T(8,128)S(1)} fusion(f32[128,2,16,128]{0,3,2,1:T(8,128)S(1)} %get-tuple-element.334, f32[2,128,16,1152]{1,3,2,0:T(8,128)} %get-tuple-element.307, f32[2,128,16]{1,2,0:T(8,128)S(1)} %get-tuple-element.308, f32[128,2,16]{0,2,1:T(8,128)S(1)} %bitcast.65, f32[128,2,16]{0,2,1:T(8,128)S(1)} %get-tuple-element.311, ...), kind=kOutput, calls=%fused_computation.9.clone.1 | convolution fusion | flops 1221066752 | bytes 23724544 | tf_op jit(solution)/shard_map/while/body/eval_jaxpr/hqrk,khd->qhrd/dot_general | solution.py:18
  259.3 8.9 %fusion.33 = (f32[2,128,16]{1,2,0:T(8,128)S(1)}, f32[2,128,16,1152]{1,3,2,0:T(8,128)}) fusion(bf16[128,2,16,128]{3,0,2,1:T(8,128)(2,1)S(1)} %get-tuple-element.359, bf16[8,1152,2,128]{3,1,0,2:T(8,128)(2,1)} %get-tuple-element.358, s32[]{:T(128)} %get-tuple-element.331, pred[128,1152]{0,1:T(8,128)(4,1)S(1)} %pad_add_fusion.2), kind=kOutput, calls=%fused_computation.30.clone.1 | convolution fusion | flops 1222111232 | bytes 20677120 | tf_op jit(solution)/shard_map/while/body/eval_jaxpr/qhrd,khd->hqrk/dot_general | solution.py:11
  268.2 9.2 %fusion.34 = f32[2,128,16]{1,2,0:T(8,128)S(1)} fusion(f32[2,128,16,1152]{1,3,2,0:T(8,128)} %get-tuple-element.307, f32[2,128,16]{1,2,0:T(8,128)S(1)} %get-tuple-element.308), kind=kLoop, calls=%fused_computation.3.clone.1 | loop fusion | flops 9433088 | bytes 18907136 | tf_op jit(solution)/shard_map/while/body/eval_jaxpr/reduce_sum | solution.py:17
  277.4 8.4 %fusion.36 = f32[128,2,16,128]{0,3,2,1:T(8,128)S(1)} fusion(f32[128,2,16,128]{0,3,2,1:T(8,128)S(1)} %get-tuple-element.334, f32[2,128,16,1152]{1,3,2,0:T(8,128)} %get-tuple-element.307, f32[2,128,16]{1,2,0:T(8,128)S(1)} %get-tuple-element.308, f32[128,2,16]{0,2,1:T(8,128)S(1)} %bitcast.65, f32[128,2,16]{0,2,1:T(8,128)S(1)} %get-tuple-element.311, ...), kind=kOutput, calls=%fused_computation.9.clone.1 | convolution fusion | flops 1221066752 | bytes 23724544 | tf_op jit(solution)/shard_map/while/body/eval_jaxpr/hqrk,khd->qhrd/dot_general | solution.py:18
  291.4 8.9 %fusion.33 = (f32[2,128,16]{1,2,0:T(8,128)S(1)}, f32[2,128,16,1152]{1,3,2,0:T(8,128)}) fusion(bf16[128,2,16,128]{3,0,2,1:T(8,128)(2,1)S(1)} %get-tuple-element.359, bf16[8,1152,2,128]{3,1,0,2:T(8,128)(2,1)} %get-tuple-element.358, s32[]{:T(128)} %get-tuple-element.331, pred[128,1152]{0,1:T(8,128)(4,1)S(1)} %pad_add_fusion.2), kind=kOutput, calls=%fused_computation.30.clone.1 | convolution fusion | flops 1222111232 | bytes 20677120 | tf_op jit(solution)/shard_map/while/body/eval_jaxpr/qhrd,khd->hqrk/dot_general | solution.py:11
  300.3 9.2 %fusion.34 = f32[2,128,16]{1,2,0:T(8,128)S(1)} fusion(f32[2,128,16,1152]{1,3,2,0:T(8,128)} %get-tuple-element.307, f32[2,128,16]{1,2,0:T(8,128)S(1)} %get-tuple-element.308), kind=kLoop, calls=%fused_computation.3.clone.1 | loop fusion | flops 9433088 | bytes 18907136 | tf_op jit(solution)/shard_map/while/body/eval_jaxpr/reduce_sum | solution.py:17
  309.5 8.4 %fusion.36 = f32[128,2,16,128]{0,3,2,1:T(8,128)S(1)} fusion(f32[128,2,16,128]{0,3,2,1:T(8,128)S(1)} %get-tuple-element.334, f32[2,128,16,1152]{1,3,2,0:T(8,128)} %get-tuple-element.307, f32[2,128,16]{1,2,0:T(8,128)S(1)} %get-tuple-element.308, f32[128,2,16]{0,2,1:T(8,128)S(1)} %bitcast.65, f32[128,2,16]{0,2,1:T(8,128)S(1)} %get-tuple-element.311, ...), kind=kOutput, calls=%fused_computation.9.clone.1 | convolution fusion | flops 1221066752 | bytes 23724544 | tf_op jit(solution)/shard_map/while/body/eval_jaxpr/hqrk,khd->qhrd/dot_general | solution.py:18
  323.4 8.9 %fusion.33 = (f32[2,128,16]{1,2,0:T(8,128)S(1)}, f32[2,128,16,1152]{1,3,2,0:T(8,128)}) fusion(bf16[128,2,16,128]{3,0,2,1:T(8,128)(2,1)S(1)} %get-tuple-element.359, bf16[8,1152,2,128]{3,1,0,2:T(8,128)(2,1)} %get-tuple-element.358, s32[]{:T(128)} %get-tuple-element.331, pred[128,1152]{0,1:T(8,128)(4,1)S(1)} %pad_add_fusion.2), kind=kOutput, calls=%fused_computation.30.clone.1 | convolution fusion | flops 1222111232 | bytes 20677120 | tf_op jit(solution)/shard_map/while/body/eval_jaxpr/qhrd,khd->hqrk/dot_general | solution.py:11
  332.3 9.2 %fusion.34 = f32[2,128,16]{1,2,0:T(8,128)S(1)} fusion(f32[2,128,16,1152]{1,3,2,0:T(8,128)} %get-tuple-element.307, f32[2,128,16]{1,2,0:T(8,128)S(1)} %get-tuple-element.308), kind=kLoop, calls=%fused_computation.3.clone.1 | loop fusion | flops 9433088 | bytes 18907136 | tf_op jit(solution)/shard_map/while/body/eval_jaxpr/reduce_sum | solution.py:17
  341.5 8.4 %fusion.36 = f32[128,2,16,128]{0,3,2,1:T(8,128)S(1)} fusion(f32[128,2,16,128]{0,3,2,1:T(8,128)S(1)} %get-tuple-element.334, f32[2,128,16,1152]{1,3,2,0:T(8,128)} %get-tuple-element.307, f32[2,128,16]{1,2,0:T(8,128)S(1)} %get-tuple-element.308, f32[128,2,16]{0,2,1:T(8,128)S(1)} %bitcast.65, f32[128,2,16]{0,2,1:T(8,128)S(1)} %get-tuple-element.311, ...), kind=kOutput, calls=%fused_computation.9.clone.1 | convolution fusion | flops 1221066752 | bytes 23724544 | tf_op jit(solution)/shard_map/while/body/eval_jaxpr/hqrk,khd->qhrd/dot_general | solution.py:18
  351.4 55.9 %all-gather.8.cloned.1.call-done = bf16[1024,4096]{0,1:T(8,128)(2,1)} async-done(((bf16[128,4096]{0,1:T(8,128)(2,1)}), bf16[1024,4096]{0,1:T(8,128)(2,1)}) %all-gather.8.cloned.1.call-update) | async-done | bytes 8388624 | tf_op jit(solution)/shard_map/all_gather | solution.py:100
  407.3 24.2 %fusion.19 = f32[1024,2048]{1,0:T(8,128)} fusion(bf16[1024,4096]{0,1:T(8,128)(2,1)} %all-gather.8.cloned.1.call-done, bf16[4096,2048]{1,0:T(8,128)(2,1)} %param.17), kind=kOutput, calls=%fused_computation.31 | convolution fusion | flops 17179869184 | bytes 33554432 | tf_op jit(solution)/shard_map/dot_general | solution.py:99
  434.3 141.8 %reduce-scatter.2.cloned.1.call-done = f32[256,2048]{1,0:T(8,128)} async-done(((f32[1024,2048]{1,0:T(8,128)}), f32[256,2048]{1,0:T(8,128)}) %reduce-scatter.2.cloned.1.call-update) | async-done | bytes 2097168 | tf_op jit(solution)/shard_map/reduce_scatter | solution.py:104
  576.1 2.7 convert_element_type.22
  (101 shorter events, 37.5 us)
Async XLA Ops:
  7.2 6.5 %copy-start.1 = (u32[32]{0:T(128)S(1)}, u32[32]{0:T(128)}, u32[]{:S(2)}) copy-start(u32[32]{0:T(128)} %constant.69) | copy-start | bytes 388
  7.2 45.0 %all-gather.4.cloned.1.call-start = ((), (), s32[]{:S(2)}) async-start(), calls=%async_computation.1 | async-start | bytes 5308416 | tf_op jit(solution)/shard_map/all_gather | solution.py:81
  10.1 83.5 %all-gather.6.cloned.1.call-start = ((), (), s32[]{:S(2)}) async-start(), calls=%async_computation.2 | async-start | bytes 5308416 | tf_op jit(solution)/shard_map/all_gather | solution.py:82
  13.0 394.3 %all-gather.8.cloned.1.call-start = ((), (), s32[]{:S(2)}) async-start(), calls=%async_computation.3 | async-start | bytes 9437184 | tf_op jit(solution)/shard_map/all_gather | solution.py:100
  351.2 224.9 %reduce-scatter.2.cloned.1.call-start = ((), (), s32[]{:S(2)}) async-start(), calls=%async_computation.4 | async-start | bytes 10485760 | tf_op jit(solution)/shard_map/reduce_scatter | solution.py:104
  431.5 1.2 copy-start
Sparse Core Ops, SparseCore 0:
  10.5 41.6 all-gather.3
  54.7 38.9 all-gather.5
  351.3 55.9 all-gather.7
  431.6 144.4 reduce-scatter.1
where the time goes:
time: 587 us; the launch traced here: 585 us
  waiting for transfers between devices  264 us (45%)
  matrix products  162 us (28%)
  other arithmetic  86.9 us (15%)
  local copies, waits for them, and re-layouts  26.2 us (4%)
  loops' own time  21.3 us (4%)
  between operations  14.5 us (2%)
  blocking collectives  9.46 us (2%)
    reduce_scatter x1, waiting for transfers between devices, on_device(): lax.psum_scatter(partial_sums, 'tp', scatter_dimension=0, tiled=True)  142 us
    reduce_sum x8, other arithmetic, attend(): total = jnp.sum(weights, axis=-1)  73.2 us
    dot_general x8, matrix products, attend(): jnp.einsum('qhrd,khd->hqrk', query_block, key_rows, preferred_element_typ...  71.1 us
    dot_general x8, matrix products, attend(): jnp.einsum('hqrk,khd->qhrd', weights.astype(jnp.bfloat16), value_rows, pr...  67.1 us
    all_gather x1, waiting for transfers between devices, on_device(): lax.all_gather(flat, 'ctx', axis=0, tiled=True)  55.9 us
    all_gather x1, waiting for transfers between devices, on_device(): value_piece = lax.all_gather(local_values, 'ctx', axis=0, tiled=True)  41.4 us
    all_gather x1, waiting for transfers between devices, on_device(): key_piece = lax.all_gather(local_keys, 'ctx', axis=0, tiled=True)  25.2 us
    dot_general x1, matrix products, on_device(): jnp.dot(lax.all_gather(flat, 'ctx', axis=0, tiled=True), out_weight, pref...  24.2 us
  transfers between devices with their start and end apart: 4, of which 4 were waited for; matrix products, arithmetic and copies ran while one was open for 1% of the time, Pallas kernels for 0%

commit v1 on v0

v1 whole, which is shorter than its diff:
```python
import functools
import math

import jax
import jax.numpy as jnp
from jax import lax
from jax.experimental import pallas as pl
from jax.experimental.pallas import tpu as pltpu
from jax.sharding import PartitionSpec as P

LOWEST = -1e30
KEY_BLOCK = 256
TOKEN_BLOCK = 32
CHUNKS = 2


def attention_kernel(
    counts_ref, bounds_ref, q_ref, lo_ref, k_ref, v_ref, o_ref, m_ref, acc_ref,
    *, sets, cache_rows, fresh_rows, head_rows, multiplier, first_token
):
    block = pl.program_id(1)
    tokens, group, width = q_ref.shape
    rows = tokens * group
    query = q_ref[...].reshape(rows, width)
    m_ref[...] = jnp.full(m_ref.shape, LOWEST, jnp.float32)
    acc_ref[...] = jnp.zeros(acc_ref.shape, jnp.float32)

    def update(scores, values):
        scores_max = jnp.max(scores, axis=0, keepdims=True) * multiplier
        old = m_ref[...]
        new = jnp.maximum(old, scores_max)
        m_ref[...] = new
        weights = jnp.exp2(scores * multiplier - new).astype(jnp.bfloat16)
        acc_ref[...] = acc_ref[...] * jnp.exp2(old - new) + jnp.dot(
            values, weights, preferred_element_type=jnp.float32
        )

    def score(keys):
        return lax.dot_general(
            keys, query, (((1,), (1,)), ((), ())), preferred_element_type=jnp.float32
        )

    def one_set(s, carry):
        def one_block(b, inner):
            start = pl.multiple_of(b * KEY_BLOCK, KEY_BLOCK)
            keys = k_ref[s, pl.ds(start, KEY_BLOCK), :]
            values = v_ref[s, :, pl.ds(start, KEY_BLOCK)]
            update(score(keys), values)
            return inner

        return lax.fori_loop(0, counts_ref[s], one_block, carry)

    lax.fori_loop(0, sets, one_set, 0)

    low = lo_ref[0:1, :]
    high = lo_ref[1:2, :]

    def one_fresh(s, carry):
        scores = score(k_ref[s, cache_rows : cache_rows + fresh_rows, :])
        position = s * fresh_rows + lax.broadcasted_iota(jnp.int32, scores.shape, 0)
        scores = jnp.where((position >= low) & (position <= high), scores, LOWEST)
        update(scores, v_ref[s, :, cache_rows : cache_rows + fresh_rows])
        return carry

    lax.fori_loop(bounds_ref[2 * block], bounds_ref[2 * block + 1], one_fresh, 0)
    total = acc_ref[width : width + 1, :]
    out = (acc_ref[0:width, :] / total).T
    o_ref[...] = out.astype(o_ref.dtype).reshape(tokens, group, width)


def attention(queries, first, tokens, key_sets, value_sets, counts, low, position):
    rows, heads, width = queries.shape
    sets, piece, _ = key_sets.shape
    kv_heads = key_sets.shape[2] // width
    value_rows = value_sets.shape[1] // kv_heads
    group = heads // kv_heads
    cache_rows = piece - rows
    blocks = tokens // TOKEN_BLOCK
    lanes = TOKEN_BLOCK * group
    chunk_low = low[first : first + tokens]
    chunk_position = position[first : first + tokens]
    pair = jnp.stack([chunk_low, chunk_position])
    pair = jnp.repeat(pair, group, axis=1)
    begin = chunk_low[::TOKEN_BLOCK] // rows
    end = chunk_position[TOKEN_BLOCK - 1 :: TOKEN_BLOCK] // rows + 1
    bounds = jnp.stack([begin, end], 1).reshape(-1)
    skip = first // TOKEN_BLOCK
    kernel = functools.partial(
        attention_kernel,
        sets=sets,
        cache_rows=cache_rows,
        fresh_rows=rows,
        head_rows=value_rows,
        multiplier=width**-0.5 * math.log2(math.e),
        first_token=first,
    )
    total_keys = sets * piece
    return pl.pallas_call(
        kernel,
        out_shape=jax.ShapeDtypeStruct((tokens, heads, width), jnp.bfloat16),
        grid_spec=pltpu.PrefetchScalarGridSpec(
            num_scalar_prefetch=2,
            grid=(kv_heads, blocks),
            in_specs=[
                pl.BlockSpec((TOKEN_BLOCK, group, width), lambda h, i, *_: (i + skip, h, 0)),
                pl.BlockSpec((2, lanes), lambda h, i, *_: (0, i)),
                pl.BlockSpec((sets, piece, width), lambda h, i, *_: (0, 0, h)),
                pl.BlockSpec((sets, value_rows, piece), lambda h, i, *_: (0, h, 0)),
            ],
            out_specs=pl.BlockSpec((TOKEN_BLOCK, group, width), lambda h, i, *_: (i, h, 0)),
            scratch_shapes=[
                pltpu.VMEM((1, lanes), jnp.float32),
                pltpu.VMEM((value_rows, lanes), jnp.float32),
            ],
        ),
        compiler_params=pltpu.CompilerParams(vmem_limit_bytes=48 * 1024 * 1024),
        cost_estimate=pl.CostEstimate(
            flops=4 * tokens * heads * width * total_keys,
            bytes_accessed=4 * total_keys * kv_heads * width,
            transcendentals=tokens * heads * total_keys,
        ),
    )(counts, bounds, queries, pair, key_sets, value_sets)


def pack(keys, fresh_keys, values, fresh_values, length):
    cache_rows, kv_heads, width = keys.shape
    fresh_rows = fresh_keys.shape[0]
    filled = jnp.arange(cache_rows, dtype=jnp.int32) < length
    flat_keys = keys.reshape(cache_rows, kv_heads * width)
    flat_keys = jnp.where(filled[:, None], flat_keys, flat_keys[0:1, :])
    flat_keys = jnp.concatenate([flat_keys, fresh_keys.reshape(fresh_rows, kv_heads * width)], 0)
    kept = jnp.where(filled[:, None, None], values, jnp.zeros_like(values))
    wide = jnp.concatenate([kept, fresh_values], 0).transpose(1, 2, 0)
    mask = jnp.concatenate([filled, jnp.ones((fresh_rows,), jnp.bool_)]).astype(jnp.bfloat16)
    mask = jnp.broadcast_to(mask[None, None, :], (kv_heads, 16, cache_rows + fresh_rows))
    wide = jnp.concatenate([wide, mask], 1).reshape(kv_heads * (width + 16), -1)
    return flat_keys, wide


def on_device(
    queries,
    fresh_rotated_keys,
    fresh_value_rows,
    cache_keys,
    prefix_value_rows,
    cache_lengths,
    new_segment,
    out_weight,
    *,
    ctx,
    tp,
):
    rows, heads, width = queries.shape
    kv_heads = fresh_rotated_keys.shape[1]
    cache_rows = cache_keys.shape[0]
    here = lax.axis_index("ctx")
    flat_keys, wide = pack(
        cache_keys, fresh_rotated_keys, prefix_value_rows, fresh_value_rows, cache_lengths[0]
    )
    key_sets = lax.all_gather(flat_keys, "ctx", axis=0)
    value_sets = lax.all_gather(wide, "ctx", axis=0)
    lengths = jnp.sum(value_sets[:, width, :cache_rows].astype(jnp.float32), axis=1)
    counts = (lengths.astype(jnp.int32) + KEY_BLOCK - 1) // KEY_BLOCK
    own_segment = lax.dynamic_slice_in_dim(new_segment, here * rows, rows, 0)
    low = jnp.sum((new_segment[None, :] < own_segment[:, None]).astype(jnp.int32), axis=1)
    position = here * rows + jnp.arange(rows, dtype=jnp.int32)

    step = rows // CHUNKS
    attended, mixed = [], []
    for c in range(CHUNKS):
        part = attention(
            queries, c * step, step, key_sets, value_sets, counts, low, position
        )
        attended.append(part)
        everyone = lax.all_gather(part.reshape(step, heads * width), "ctx", axis=0, tiled=True)
        sums = jnp.dot(everyone, out_weight, preferred_element_type=jnp.float32)
        sums = lax.psum_scatter(
            sums.astype(jnp.bfloat16), "tp", scatter_dimension=0, tiled=True
        )
        mixed.append(sums.reshape(ctx // tp, step, -1))
    attended = jnp.concatenate(attended, 0)
    mixed = jnp.stack(mixed, 1).reshape(ctx // tp * rows, -1)
    return attended, mixed


def solution(mesh):
    in_specs = (
        P("ctx", "tp", None),
        P("ctx", "tp", None),
        P("ctx", "tp", None),
        P("ctx", "tp", None),
        P("ctx", "tp", None),
        P("ctx"),
        P(),
        P("tp", "ctx"),
    )
    out_specs = (P("ctx", "tp", None), P("tp", "ctx"))
    return jax.shard_map(
        functools.partial(on_device, ctx=mesh.shape["ctx"], tp=mesh.shape["tp"]),
        mesh=mesh,
        in_specs=in_specs,
        out_specs=out_specs,
        check_vma=False,
    )
```

time: 587 us -> 371 us (0.63); the launches traced: 585 us -> 377 us
  matrix products: 162 us -> 29.2 us
  Pallas kernels: 0 us -> 117 us
  waiting for transfers between devices: 264 us -> 190 us
  other arithmetic: 86.9 us -> 13.5 us
  loops' own time: 21.3 us -> 0 us
  local copies, waits for them, and re-layouts: 26.2 us -> 11.1 us
  blocking collectives: 9.46 us -> 0 us
    dot_general x17 -> x2, matrix products: 162 us -> 29.2 us  [on_device(): sums = jnp.dot(everyone, out_weight, preferred_element_type=jnp.float32)]
    pallas_call x0 -> x2, Pallas kernels: none -> 117 us  [attention(): pl.pallas_call(kernel, out_shape=jax.ShapeDtypeStruct((tokens, heads, wid...]
    reduce_sum x8 -> x2, other arithmetic: 73.2 us -> 1.26 us  [the longest x1 1.06 us: on_device(): jnp.sum(value_sets[:, width, :cache_rows].astype(jnp.float32), axis=1)]
    reduce_scatter x1 -> x2, waiting for transfers between devices: 142 us -> 75.7 us  [on_device(): lax.psum_scatter(sums.astype(jnp.bfloat16), 'tp', scatter_dimension=0, ti...]
    another operation x1 -> x0, loops' own time: 21.3 us -> none  [on_device(): lax.scan(step, state, (key_stack, value_stack, jnp.arange(count, dtype=jn...]
    dynamic_slice x25 -> x1, local copies, waits for them, and re-layouts: 16.3 us -> 0.07 us  [on_device(): own_segment = lax.dynamic_slice_in_dim(new_segment, here * rows, rows, 0)]
    unnamed x1 -> x0, blocking collectives: 9.46 us -> none
    all_gather x3 -> x4, waiting for transfers between devices: 122 us -> 114 us  [the longest x1 42 us: on_device(): value_sets = lax.all_gather(wide, 'ctx', axis=0)]
  transfers between devices with their start and end apart: 4 -> 6, of which waited for: 4 -> 5; matrix products, arithmetic and copies ran while one was open for 1% -> 9% of each run, Pallas kernels for 0% -> 16%
where the time goes in v1:
time: 371 us; the launch traced here: 377 us
  waiting for transfers between devices  190 us (51%)
  Pallas kernels  117 us (32%)
  matrix products  29.2 us (8%)
  between operations  15 us (4%)
  other arithmetic  13.5 us (4%)
  local copies, waits for them, and re-layouts  11.1 us (3%)
    pallas_call x2, Pallas kernels, attention(): pl.pallas_call(kernel, out_shape=jax.ShapeDtypeStruct((tokens, heads, wid...  117 us
    reduce_scatter x2, waiting for transfers between devices, on_device(): lax.psum_scatter(sums.astype(jnp.bfloat16), 'tp', scatter_dimension=0, ti...  75.7 us
    all_gather x1, waiting for transfers between devices, on_device(): value_sets = lax.all_gather(wide, 'ctx', axis=0)  42 us
    all_gather x1, waiting for transfers between devices, on_device(): key_sets = lax.all_gather(flat_keys, 'ctx', axis=0)  40.3 us
    all_gather x2, waiting for transfers between devices, on_device(): lax.all_gather(part.reshape(step, heads * width), 'ctx', axis=0, tiled=True)  32.2 us
    dot_general x2, matrix products, on_device(): sums = jnp.dot(everyone, out_weight, preferred_element_type=jnp.float32)  29.2 us
  transfers between devices with their start and end apart: 6, of which 5 were waited for; matrix products, arithmetic and copies ran while one was open for 9% of the time, Pallas kernels for 16%

profile of v1, /device:TPU:0, one launch (start us, length us, event | category | flops | bytes accessed | tf_op | source)
XLA Modules:
  0.0 376.8 jit_solution(16110769012468618499)
XLA Ops:
  8.0 5.2 %broadcast_select_fusion = bf16[1024,2,128]{2,1,0:T(2,128)(2,1)S(1)} fusion(bf16[1024,2,128]{2,1,0:T(2,128)(2,1)} %param.12, pred[1024]{0:T(1024)(128)(4,1)S(1)} %iota_compare_fusion), kind=kLoop, calls=%fused_computation.5 | loop fusion | flops 262144 | bytes 1049600 | tf_op jit(solution)/shard_map/jit(_where)/select_n | solution.py:132
  13.2 2.1 maximum_bitcast_fusion
  15.3 3.9 %broadcast_in_dim.48 = bf16[2,16,1152]{1,0,2:T(2,128)(2,1)S(1)} broadcast(bf16[1152]{0:T(1024)(128)(2,1)S(1)} %pad_convert_fusion), dimensions={2} | broadcast | bytes 76032 | tf_op jit(solution)/shard_map/broadcast_in_dim | solution.py:135
  19.1 1.5 pad_maximum_fusion
  20.6 2.8 copy.22
  23.5 0.2 bitcast_select_fusion
  23.7 0.9 pad_maximum_fusion.3
  24.8 0.1 slice.40
  24.9 0.2 convert_reduce_fusion
  25.2 0.1 slice.38
  25.4 0.1 copy.24
  25.6 0.1 reshape.50.lo_ref
  25.7 42.0 %all-gather.6.cloned.1.call-done.v_ref = bf16[8,288,1152]{2,1,0:T(8,128)(2,1)} async-done(((bf16[1,288,1152]{2,1,0:T(8,128)(2,1)}), bf16[8,288,1152]{2,1,0:T(8,128)(2,1)}) %all-gather.6.cloned.1.call-update) | async-done | bytes 5308432 | tf_op jit(solution)/shard_map/all_gather | solution.py:161
  67.7 1.1 fusion
  68.8 40.3 %all-gather.12.cloned.1.call-done = bf16[9216,256]{1,0:T(8,128)(2,1)} async-done(((bf16[1152,256]{1,0:T(8,128)(2,1)}), bf16[9216,256]{1,0:T(8,128)(2,1)}) %all-gather.12.cloned.1.call-update) | async-done | bytes 4718608 | tf_op jit(solution)/shard_map/all_gather | solution.py:160
  109.1 58.6 %shard_map.96 = bf16[64,32,128]{2,1,0:T(8,128)(2,1)S(1)} custom-call(s32[8]{0:T(128)S(1)} %and_select_fusion.4.counts_ref, s32[4]{0:T(128)S(1)} %reshape.49.bounds_ref, bf16[128,32,128]{2,1,0:T(8,128)(2,1)S(1)} %copy-done, s32[2,1024]{1,0:T(2,128)S(1)} %reshape.50.lo_ref, bf16[8,1152,256]{2,1,0:T(8,128)(2,1)} %bitcast.57, ...), custom_call_target="tpu_custom_call" | custom-call | flops 9663676416 | bytes 9437184 | tf_op jit(solution)/shard_map/pallas_call | solution.py:98
  167.7 1.0 copy.34
  168.8 0.1 slice.35
  168.9 0.1 slice.33
  169.0 0.1 copy.23
  169.3 0.1 reshape.46.lo_ref
  169.4 58.6 %shard_map.95 = bf16[64,32,128]{2,1,0:T(8,128)(2,1)S(1)} custom-call(s32[8]{0:T(128)S(1)} %and_select_fusion.4.counts_ref, s32[4]{0:T(128)S(1)} %reshape.45.bounds_ref, bf16[128,32,128]{2,1,0:T(8,128)(2,1)S(1)} %copy-done, s32[2,1024]{1,0:T(2,128)S(1)} %reshape.46.lo_ref, bf16[8,1152,256]{2,1,0:T(8,128)(2,1)} %bitcast.58, ...), custom_call_target="tpu_custom_call" | custom-call | flops 9663676416 | bytes 9437184 | tf_op jit(solution)/shard_map/pallas_call | solution.py:98
  228.0 1.0 copy.35
  229.2 14.6 %convolution_convert_fusion = bf16[512,2048]{1,0:T(8,128)(2,1)} fusion(bf16[512,4096]{1,0:T(8,128)(2,1)} %all-gather.10.cloned.1.call-done, bf16[4096,2048]{1,0:T(8,128)(2,1)} %param.15), kind=kOutput, calls=%fused_computation | convolution fusion | flops 8590983168 | bytes 23068672 | tf_op jit(solution)/shard_map/dot_general | solution.py:176
  243.8 0.2 reduce-scatter.3.cloned.1.call-start
  244.0 32.2 %all-gather.8.cloned.1.call-done = bf16[512,4096]{1,0:T(8,128)(2,1)} async-done(((bf16[64,4096]{1,0:T(8,128)(2,1)}), bf16[512,4096]{1,0:T(8,128)(2,1)}) %all-gather.8.cloned.1.call-update) | async-done | bytes 4194320 | tf_op jit(solution)/shard_map/all_gather | solution.py:175
  276.2 14.6 %convolution_convert_fusion.1 = bf16[512,2048]{1,0:T(8,128)(2,1)} fusion(bf16[512,4096]{1,0:T(8,128)(2,1)} %all-gather.8.cloned.1.call-done, bf16[4096,2048]{1,0:T(8,128)(2,1)} %param.15), kind=kOutput, calls=%fused_computation.1 | convolution fusion | flops 8590983168 | bytes 23068672 | tf_op jit(solution)/shard_map/dot_general | solution.py:176
  290.8 1.1 pad_maximum_fusion.1
  291.8 30.3 %reduce-scatter.5.cloned.1.call-done = bf16[128,2048]{1,0:T(8,128)(2,1)} async-done(((bf16[512,2048]{1,0:T(8,128)(2,1)}), bf16[128,2048]{1,0:T(8,128)(2,1)}) %reduce-scatter.5.cloned.1.call-update) | async-done | bytes 524304 | tf_op jit(solution)/shard_map/reduce_scatter | solution.py:177
  322.2 45.4 %reduce-scatter.3.cloned.1.call-done = bf16[128,2048]{1,0:T(8,128)(2,1)} async-done(((bf16[512,2048]{1,0:T(8,128)(2,1)}), bf16[128,2048]{1,0:T(8,128)(2,1)}) %reduce-scatter.3.cloned.1.call-update) | async-done | bytes 524304 | tf_op jit(solution)/shard_map/reduce_scatter | solution.py:177
  367.6 1.3 pad_maximum_fusion.2
  368.9 1.1 copy.25
  (38 shorter events, 1.0 us)
Async XLA Ops:
  7.2 16.3 %copy-start.2 = (bf16[128,2,128]{2,1,0:T(2,128)(2,1)S(1)}, bf16[128,2,128]{2,1,0:T(2,128)(2,1)}, u32[]{:S(2)}) copy-start(bf16[128,2,128]{2,1,0:T(2,128)(2,1)} %param.9) | copy-start | bytes 196612
  7.2 16.3 %copy-start.1 = (bf16[1024,2,128]{2,1,0:T(2,128)(2,1)S(1)}, bf16[1024,2,128]{2,1,0:T(2,128)(2,1)}, u32[]{:S(2)}) copy-start(bf16[1024,2,128]{2,1,0:T(2,128)(2,1)} %param.11) | copy-start | bytes 1572868
  7.2 60.5 %all-gather.6.cloned.1.call-start = ((), (), s32[]{:S(2)}) async-start(), calls=%async_computation.2 | async-start | bytes 5971968 | tf_op jit(solution)/shard_map/all_gather | solution.py:161
  15.2 9.6 %copy-start.3 = (s32[1024]{0:T(1024)S(1)}, s32[1024]{0:T(1024)}, u32[]{:S(2)}) copy-start(s32[1024]{0:T(1024)} %param.14) | copy-start | bytes 12292
  15.2 93.8 %copy-start = (bf16[128,32,128]{2,1,0:T(8,128)(2,1)S(1)}, bf16[128,32,128]{2,1,0:T(8,128)(2,1)}, u32[]{:S(2)}) copy-start(bf16[128,32,128]{2,1,0:T(8,128)(2,1)} %q_ref.3) | copy-start | bytes 3145732
  23.4 85.7 %all-gather.12.cloned.1.call-start = ((), (), s32[]{:S(2)}) async-start(), calls=%async_computation.7 | async-start | bytes 5308416 | tf_op jit(solution)/shard_map/all_gather | solution.py:160
  24.6 204.5 %all-gather.10.cloned.1.call-start = ((), (), s32[]{:S(2)}) async-start(), calls=%async_computation.5 | async-start | bytes 4718592 | tf_op jit(solution)/shard_map/all_gather | solution.py:175
  168.8 107.4 %all-gather.8.cloned.1.call-start = ((), (), s32[]{:S(2)}) async-start(), calls=%async_computation.3 | async-start | bytes 4718592 | tf_op jit(solution)/shard_map/all_gather | solution.py:175
  229.1 93.1 %reduce-scatter.5.cloned.1.call-start = ((), (), s32[]{:S(2)}) async-start(), calls=%async_computation.6 | async-start | bytes 2621440 | tf_op jit(solution)/shard_map/reduce_scatter | solution.py:177
  243.8 123.8 %reduce-scatter.3.cloned.1.call-start = ((), (), s32[]{:S(2)}) async-start(), calls=%async_computation.4 | async-start | bytes 2621440 | tf_op jit(solution)/shard_map/reduce_scatter | solution.py:177
Sparse Core Ops, SparseCore 0:
  23.6 44.0 all-gather.5
  70.1 38.9 all-gather.11
  168.9 41.8 all-gather.9
  229.2 46.9 all-gather.7
  278.3 43.8 reduce-scatter.4
  324.4 43.1 reduce-scatter.2

commit v2 on v1

--- a/solution.py
+++ b/solution.py
@@ -10,35 +10,47 @@
 
 LOWEST = -1e30
 KEY_BLOCK = 256
-TOKEN_BLOCK = 32
+TOKEN_BLOCK = 64
+LANES = 256
 CHUNKS = 2
 
 
 def attention_kernel(
     counts_ref, bounds_ref, q_ref, lo_ref, k_ref, v_ref, o_ref, m_ref, acc_ref,
-    *, sets, cache_rows, fresh_rows, head_rows, multiplier, first_token
+    *, sets, cache_rows, fresh_rows, multiplier
 ):
     block = pl.program_id(1)
     tokens, group, width = q_ref.shape
     rows = tokens * group
-    query = q_ref[...].reshape(rows, width)
     m_ref[...] = jnp.full(m_ref.shape, LOWEST, jnp.float32)
     acc_ref[...] = jnp.zeros(acc_ref.shape, jnp.float32)
-
-    def update(scores, values):
-        scores_max = jnp.max(scores, axis=0, keepdims=True) * multiplier
-        old = m_ref[...]
-        new = jnp.maximum(old, scores_max)
-        m_ref[...] = new
-        weights = jnp.exp2(scores * multiplier - new).astype(jnp.bfloat16)
-        acc_ref[...] = acc_ref[...] * jnp.exp2(old - new) + jnp.dot(
-            values, weights, preferred_element_type=jnp.float32
-        )
+    part_tokens = LANES // group
+    parts = [(pl.ds(p * LANES, LANES), p * part_tokens) for p in range(rows // LANES)]
+
+    def update(all_scores, values):
+        olds = [m_ref[:, lanes] for lanes, _ in parts]
+        news = [
+            jnp.maximum(old, jnp.max(scores, axis=0, keepdims=True) * multiplier)
+            for old, scores in zip(olds, all_scores)
+        ]
+        sums = []
+        for scores, new in zip(all_scores, news):
+            weights = jnp.exp2(scores * multiplier - new).astype(jnp.bfloat16)
+            sums.append(jnp.dot(values, weights, preferred_element_type=jnp.float32))
+        for (lanes, _), old, new, part in zip(parts, olds, news, sums):
+            m_ref[:, lanes] = new
+            acc_ref[:, lanes] = acc_ref[:, lanes] * jnp.exp2(old - new) + part
 
     def score(keys):
-        return lax.dot_general(
-            keys, query, (((1,), (1,)), ((), ())), preferred_element_type=jnp.float32
-        )
+        return [
+            lax.dot_general(
+                keys,
+                q_ref[start : start + part_tokens].reshape(LANES, width),
+                (((1,), (1,)), ((), ())),
+                preferred_element_type=jnp.float32,
+            )
+            for _, start in parts
+        ]
 
     def one_set(s, carry):
         def one_block(b, inner):
@@ -52,20 +64,109 @@
 
     lax.fori_loop(0, sets, one_set, 0)
 
-    low = lo_ref[0:1, :]
-    high = lo_ref[1:2, :]
-
     def one_fresh(s, carry):
+        all_scores = []
+        first = s * fresh_rows
         scores = score(k_ref[s, cache_rows : cache_rows + fresh_rows, :])
-        position = s * fresh_rows + lax.broadcasted_iota(jnp.int32, scores.shape, 0)
-        scores = jnp.where((position >= low) & (position <= high), scores, LOWEST)
-        update(scores, v_ref[s, :, cache_rows : cache_rows + fresh_rows])
+        for (lanes, _), part in zip(parts, scores):
+            place = first + lax.broadcasted_iota(jnp.int32, part.shape, 0)
+            seen = (place >= lo_ref[0:1, lanes]) & (place <= lo_ref[1:2, lanes])
+            all_scores.append(jnp.where(seen, part, LOWEST))
+        update(all_scores, v_ref[s, :, cache_rows : cache_rows + fresh_rows])
         return carry
 
     lax.fori_loop(bounds_ref[2 * block], bounds_ref[2 * block + 1], one_fresh, 0)
-    total = acc_ref[width : width + 1, :]
-    out = (acc_ref[0:width, :] / total).T
-    o_ref[...] = out.astype(o_ref.dtype).reshape(tokens, group, width)
+    for lanes, start in parts:
+        total = acc_ref[width : width + 1, lanes]
+        out = (acc_ref[0:width, lanes] / total).T
+        o_ref[start : start + part_tokens] = out.astype(o_ref.dtype).reshape(
+            part_tokens, group, width
+        )
+
+
+def gather_kernel(a_ref, b_ref, a_out, b_out, local_sem, send_sem, recv_sem):
+    me = lax.axis_index("ctx")
+    column = lax.rem(me // 2, 2)
+    line = me // 4
+    along_x = me + 2 - 4 * column
+    along_y = me + 4 - 8 * line
+    across = along_y + 2 - 4 * column
+    core = lax.rem(me, 2)
+    other = me + 1 - 2 * core
+
+    barrier = pltpu.get_barrier_semaphore()
+    for partner in (along_x, along_y, other):
+        pl.semaphore_signal(
+            barrier, inc=1, device_id={"ctx": partner}, device_id_type=pl.DeviceIdType.MESH
+        )
+    pl.semaphore_wait(barrier, 3)
+
+    def send(which, slot, source, owner, partner):
+        out = (a_out, b_out)[which]
+        copy = pltpu.make_async_remote_copy(
+            src_ref=source,
+            dst_ref=out.at[owner],
+            send_sem=send_sem.at[which, slot],
+            recv_sem=recv_sem.at[which, slot],
+            device_id={"ctx": partner},
+            device_id_type=pl.DeviceIdType.MESH,
+        )
+        copy.start()
+        return copy
+
+    copies = []
+    keep = []
+    for which, (source, out) in enumerate(((a_ref, a_out), (b_ref, b_out))):
+        by_x = send(which, 0, source, me, along_x)
+        by_y = send(which, 1, source, me, along_y)
+        inside = send(which, 2, source, me, other)
+        copies.append([by_x, by_y, inside])
+        local = pltpu.make_async_copy(source, out.at[me], local_sem.at[which])
+        local.start()
+        keep.append(local)
+
+    a_copies, b_copies = copies
+    a_copies[0].wait_recv()
+    a_copies.append(send(0, 3, a_out.at[along_x], along_x, along_y))
+    a_copies.append(send(0, 4, a_out.at[along_x], along_x, other))
+    b_copies[1].wait_recv()
+    b_copies.append(send(1, 3, b_out.at[along_y], along_y, along_x))
+    b_copies.append(send(1, 4, b_out.at[along_y], along_y, other))
+    a_copies[1].wait_recv()
+    a_copies.append(send(0, 5, a_out.at[along_y], along_y, other))
+    b_copies[0].wait_recv()
+    b_copies.append(send(1, 5, b_out.at[along_x], along_x, other))
+    a_copies[3].wait_recv()
+    a_copies.append(send(0, 6, a_out.at[across], across, other))
+    b_copies[3].wait_recv()
+    b_copies.append(send(1, 6, b_out.at[across], across, other))
+    for group in copies:
+        for slot in (2, 4, 5, 6):
+            group[slot].wait_recv()
+        for copy in group:
+            copy.wait_send()
+    for local in keep:
+        local.wait()
+
+
+def gather_pair(a, b, ctx, collective_id):
+    if ctx != 8:
+        return lax.all_gather(a, "ctx", axis=0), lax.all_gather(b, "ctx", axis=0)
+    return pl.pallas_call(
+        gather_kernel,
+        out_shape=[jax.ShapeDtypeStruct((ctx,) + x.shape, x.dtype) for x in (a, b)],
+        in_specs=[pl.BlockSpec(memory_space=pl.ANY)] * 2,
+        out_specs=[pl.BlockSpec(memory_space=pl.ANY)] * 2,
+        scratch_shapes=[
+            pltpu.SemaphoreType.DMA((2,)),
+            pltpu.SemaphoreType.DMA((2, 7)),
+            pltpu.SemaphoreType.DMA((2, 7)),
+        ],
+        compiler_params=pltpu.CompilerParams(collective_id=collective_id, has_side_effects=True),
+        cost_estimate=pl.CostEstimate(
+            flops=0, bytes_accessed=16 * (a.size + b.size), transcendentals=0
+        ),
+    )(a, b)
 
 
 def attention(queries, first, tokens, key_sets, value_sets, counts, low, position):
@@ -90,9 +191,7 @@
         sets=sets,
         cache_rows=cache_rows,
         fresh_rows=rows,
-        head_rows=value_rows,
         multiplier=width**-0.5 * math.log2(math.e),
-        first_token=first,
     )
     total_keys = sets * piece
     return pl.pallas_call(
@@ -157,8 +256,7 @@
     flat_keys, wide = pack(
         cache_keys, fresh_rotated_keys, prefix_value_rows, fresh_value_rows, cache_lengths[0]
     )
-    key_sets = lax.all_gather(flat_keys, "ctx", axis=0)
-    value_sets = lax.all_gather(wide, "ctx", axis=0)
+    key_sets, value_sets = gather_pair(flat_keys, wide, ctx, 0)
     lengths = jnp.sum(value_sets[:, width, :cache_rows].astype(jnp.float32), axis=1)
     counts = (lengths.astype(jnp.int32) + KEY_BLOCK - 1) // KEY_BLOCK
     own_segment = lax.dynamic_slice_in_dim(new_segment, here * rows, rows, 0)
@@ -172,11 +270,15 @@
             queries, c * step, step, key_sets, value_sets, counts, low, position
         )
         attended.append(part)
-        everyone = lax.all_gather(part.reshape(step, heads * width), "ctx", axis=0, tiled=True)
+        flat = part.reshape(step, heads * width)
+        halves = gather_pair(flat[: step // 2], flat[step // 2 :], ctx, c + 1)
+        everyone = jnp.concatenate(halves, 1).reshape(ctx * step, heads * width)
+        if mixed:
+            everyone, mixed[-1] = lax.optimization_barrier((everyone, mixed[-1]))
         sums = jnp.dot(everyone, out_weight, preferred_element_type=jnp.float32)
-        sums = lax.psum_scatter(
-            sums.astype(jnp.bfloat16), "tp", scatter_dimension=0, tiled=True
-        )
+        sums = sums.astype(jnp.bfloat16)
+        queries, sums = lax.optimization_barrier((queries, sums))
+        sums = lax.psum_scatter(sums, "tp", scatter_dimension=0, tiled=True)
         mixed.append(sums.reshape(ctx // tp, step, -1))
     attended = jnp.concatenate(attended, 0)
     mixed = jnp.stack(mixed, 1).reshape(ctx // tp * rows, -1)

time: 371 us -> 304 us (0.82); the launches traced: 377 us -> 300 us
  waiting for transfers between devices: 190 us -> 42.9 us
  Pallas kernels: 117 us -> 168 us
  between operations: 15 us -> 24.9 us
  other arithmetic: 13.5 us -> 21.5 us
  local copies, waits for them, and re-layouts: 11.1 us -> 15.1 us
    all_gather x4 -> x0, waiting for transfers between devices: 114 us -> none  [the longest x1 42 us: on_device(): value_sets = lax.all_gather(wide, 'ctx', axis=0)]
    pallas_call x0 -> x3, Pallas kernels: none -> 102 us  [gather_pair(): pl.pallas_call(gather_kernel, out_shape=[jax.ShapeDtypeStruct((ctx,) + x....]
    pallas_call x2, Pallas kernels: 117 us -> 65.6 us  [attention(): pl.pallas_call(kernel, out_shape=jax.ShapeDtypeStruct((tokens, heads, wid...]
    reduce_scatter x2, waiting for transfers between devices: 75.7 us -> 42.8 us  [on_device(): sums = lax.psum_scatter(sums, 'tp', scatter_dimension=0, tiled=True)]
    concatenate x0 -> x2, other arithmetic: none -> 7.38 us  [on_device(): everyone = jnp.concatenate(halves, 1).reshape(ctx * step, heads * width)]
  transfers between devices with their start and end apart: 6 -> 2, of which waited for: 5 -> 1; matrix products, arithmetic and copies ran while one was open for 9% -> 3% of each run, Pallas kernels for 16% -> 19%
where the time goes in v2:
time: 304 us; the launch traced here: 300 us
  Pallas kernels  168 us (55%)
  waiting for transfers between devices  42.9 us (14%)
  matrix products  27.9 us (9%)
  between operations  24.9 us (8%)
  other arithmetic  21.5 us (7%)
  local copies, waits for them, and re-layouts  15.1 us (5%)
    pallas_call x3, Pallas kernels, gather_pair(): pl.pallas_call(gather_kernel, out_shape=[jax.ShapeDtypeStruct((ctx,) + x....  102 us
    pallas_call x2, Pallas kernels, attention(): pl.pallas_call(kernel, out_shape=jax.ShapeDtypeStruct((tokens, heads, wid...  65.6 us
    reduce_scatter x2, waiting for transfers between devices, on_device(): sums = lax.psum_scatter(sums, 'tp', scatter_dimension=0, tiled=True)  42.8 us
    dot_general x2, matrix products, on_device(): sums = jnp.dot(everyone, out_weight, preferred_element_type=jnp.float32)  27.9 us
    concatenate x2, other arithmetic, on_device(): everyone = jnp.concatenate(halves, 1).reshape(ctx * step, heads * width)  7.38 us
  transfers between devices with their start and end apart: 2, of which 1 were waited for; matrix products, arithmetic and copies ran while one was open for 3% of the time, Pallas kernels for 19%

profile of v2, /device:TPU:0, one launch (start us, length us, event | category | flops | bytes accessed | tf_op | source)
XLA Modules:
  0.0 300.4 jit_solution(9313336004177372008)
XLA Ops:
  7.2 0.6 fusion.3
  9.1 0.8 dynamic_slice.3
  9.9 0.9 convert_reduce_fusion
  10.8 0.6 fusion.2
  15.4 0.8 copy.32
  16.9 0.7 slice_bitcast_fusion.4
  17.6 5.2 %broadcast_select_fusion = bf16[1024,2,128]{2,1,0:T(2,128)(2,1)S(1)} fusion(bf16[1024,2,128]{2,1,0:T(2,128)(2,1)} %param.12, pred[1024]{0:T(1024)(128)(4,1)S(1)} %iota_compare_fusion), kind=kLoop, calls=%fused_computation.7 | loop fusion | flops 262144 | bytes 1049600 | tf_op jit(solution)/shard_map/jit(_where)/select_n | solution.py:231
  22.8 2.1 maximum_bitcast_fusion
  24.9 3.9 %broadcast_in_dim.51 = bf16[2,16,1152]{1,0,2:T(2,128)(2,1)S(1)} broadcast(bf16[1152]{0:T(1024)(128)(2,1)S(1)} %pad_convert_fusion), dimensions={2} | broadcast | bytes 76032 | tf_op jit(solution)/shard_map/broadcast_in_dim | solution.py:234
  28.8 1.5 pad_maximum_fusion.2
  30.2 2.8 copy.14
  33.0 0.2 bitcast_select_fusion
  33.3 0.9 pad_maximum_fusion.5.a_ref
  34.1 50.2 %shard_map.95 = (bf16[8,1152,256]{2,1,0:T(8,128)(2,1)}, bf16[8,288,1152]{2,1,0:T(8,128)(2,1)}) custom-call(bf16[1152,256]{1,0:T(8,128)(2,1)} %pad_maximum_fusion.5.a_ref, bf16[288,1152]{1,0:T(8,128)(2,1)} %bitcast.58), custom_call_target="tpu_custom_call" | custom-call | bytes 10027008 | tf_op jit(solution)/shard_map/pallas_call | solution.py:155
  84.3 1.1 convert_reduce_fusion.1
  85.7 32.8 %shard_map.96 = bf16[64,32,128]{2,1,0:T(8,128)(2,1)S(1)} custom-call(s32[8]{0:T(128)S(1)} %and_select_fusion.counts_ref, s32[2]{0:T(128)S(1)} %add_bitcast_fusion.bounds_ref, bf16[128,32,128]{2,1,0:T(8,128)(2,1)S(1)} %copy-done, s32[2,1024]{1,0:T(2,128)S(1)} %reshape.77.lo_ref, bf16[8,1152,256]{2,1,0:T(8,128)(2,1)} %get-tuple-element.14.k_ref, ...), custom_call_target="tpu_custom_call" | custom-call | flops 9663676416 | bytes 9437184 | tf_op jit(solution)/shard_map/pallas_call | solution.py:197
  118.6 0.8 copy.31
  119.4 0.8 copy.30
  120.2 26.8 %shard_map.97 = (bf16[8,32,4096]{2,1,0:T(8,128)(2,1)}, bf16[8,32,4096]{2,1,0:T(8,128)(2,1)}) custom-call(bf16[32,4096]{1,0:T(8,128)(2,1)} %bitcast.60, bf16[32,4096]{1,0:T(8,128)(2,1)} %bitcast.62), custom_call_target="tpu_custom_call" | custom-call | bytes 4194304 | tf_op jit(solution)/shard_map/pallas_call | solution.py:155
  147.0 2.7 pad_maximum_fusion
  149.7 13.4 %convolution_convert_fusion.1 = bf16[512,2048]{1,0:T(8,128)(2,1)} fusion(bf16[512,4096]{1,0:T(8,128)(2,1)S(1)} %bitcast.57, bf16[4096,2048]{1,0:T(8,128)(2,1)} %param.15), kind=kOutput, calls=%fused_computation.3 | convolution fusion | flops 8590983168 | bytes 23068672 | tf_op jit(solution)/shard_map/dot_general | solution.py:278
  163.1 0.2 reduce-scatter.5.cloned.1.call-start
  168.4 32.9 %shard_map.98 = bf16[64,32,128]{2,1,0:T(8,128)(2,1)S(1)} custom-call(s32[8]{0:T(128)S(1)} %and_select_fusion.counts_ref, s32[2]{0:T(128)S(1)} %add_bitcast_fusion.1.bounds_ref, bf16[128,32,128]{2,1,0:T(8,128)(2,1)S(1)} %copy-done, s32[2,1024]{1,0:T(2,128)S(1)} %reshape.80.lo_ref, bf16[8,1152,256]{2,1,0:T(8,128)(2,1)} %get-tuple-element.14.k_ref, ...), custom_call_target="tpu_custom_call" | custom-call | flops 9663676416 | bytes 9437184 | tf_op jit(solution)/shard_map/pallas_call | solution.py:197
  201.4 0.8 copy.29
  202.2 0.8 copy.28
  203.0 25.2 %shard_map.99 = (bf16[8,32,4096]{2,1,0:T(8,128)(2,1)}, bf16[8,32,4096]{2,1,0:T(8,128)(2,1)}) custom-call(bf16[32,4096]{1,0:T(8,128)(2,1)} %bitcast.61, bf16[32,4096]{1,0:T(8,128)(2,1)} %bitcast.63), custom_call_target="tpu_custom_call" | custom-call | bytes 4194304 | tf_op jit(solution)/shard_map/pallas_call | solution.py:155
  228.2 4.7 %pad_maximum_fusion.1 = bf16[8,64,4096]{2,1,0:T(8,128)(2,1)} fusion(bf16[8,32,4096]{2,1,0:T(8,128)(2,1)} %get-tuple-element.19, bf16[8,32,4096]{2,1,0:T(8,128)(2,1)} %get-tuple-element.18), kind=kLoop, calls=%fused_computation.1 | loop fusion | flops 8388608 | bytes 8388608 | tf_op jit(solution)/shard_map/concatenate | solution.py:275
  232.9 14.6 %convolution_convert_fusion = bf16[512,2048]{1,0:T(8,128)(2,1)} fusion(bf16[512,4096]{1,0:T(8,128)(2,1)} %bitcast.56, bf16[4096,2048]{1,0:T(8,128)(2,1)} %param.15), kind=kOutput, calls=%fused_computation.2 | convolution fusion | flops 8590983168 | bytes 23068672 | tf_op jit(solution)/shard_map/dot_general | solution.py:278
  247.5 1.1 pad_maximum_fusion.3
  248.5 42.8 %reduce-scatter.5.cloned.1.call-done = bf16[128,2048]{1,0:T(8,128)(2,1)} async-done(((bf16[512,2048]{1,0:T(8,128)(2,1)}), bf16[128,2048]{1,0:T(8,128)(2,1)}) %reduce-scatter.5.cloned.1.call-update) | async-done | bytes 524304 | tf_op jit(solution)/shard_map/reduce_scatter | solution.py:281
  291.4 1.1 pad_maximum_fusion.4
  292.5 1.1 copy.15
  (25 shorter events, 0.9 us)
Async XLA Ops:
  7.2 25.9 %copy-start.1 = (bf16[1024,2,128]{2,1,0:T(2,128)(2,1)S(1)}, bf16[1024,2,128]{2,1,0:T(2,128)(2,1)}, u32[]{:S(2)}) copy-start(bf16[1024,2,128]{2,1,0:T(2,128)(2,1)} %param.11) | copy-start | bytes 1572868
  7.2 225.7 %reduce-scatter.3.cloned.1.call-start = ((), (), s32[]{:S(2)}) async-start(), calls=%async_computation.2 | async-start | bytes 2621440 | tf_op jit(solution)/shard_map/reduce_scatter | solution.py:281
  24.9 60.8 %copy-start = (bf16[128,32,128]{2,1,0:T(8,128)(2,1)S(1)}, bf16[128,32,128]{2,1,0:T(8,128)(2,1)}, u32[]{:S(2)}) copy-start(bf16[128,32,128]{2,1,0:T(8,128)(2,1)} %q_ref.2) | copy-start | bytes 3145732
  163.1 128.3 %reduce-scatter.5.cloned.1.call-start = ((), (), s32[]{:S(2)}) async-start(), calls=%async_computation.3 | async-start | bytes 2621440 | tf_op jit(solution)/shard_map/reduce_scatter | solution.py:281
  247.5 43.9 %copy-start.2 = (bf16[128,2048]{1,0:T(8,128)(2,1)S(1)}, bf16[128,2048]{1,0:T(8,128)(2,1)}, u32[]{:S(2)}) copy-start(bf16[128,2048]{1,0:T(8,128)(2,1)} %reduce-scatter.3.cloned.1.call-done) | copy-start | bytes 1572868
Sparse Core Ops, SparseCore 0:
  163.2 43.8 reduce-scatter.2
  247.6 43.7 reduce-scatter.4

commit v3 on v2

--- a/solution.py
+++ b/solution.py
@@ -228,8 +228,13 @@
     flat_keys = keys.reshape(cache_rows, kv_heads * width)
     flat_keys = jnp.where(filled[:, None], flat_keys, flat_keys[0:1, :])
     flat_keys = jnp.concatenate([flat_keys, fresh_keys.reshape(fresh_rows, kv_heads * width)], 0)
-    kept = jnp.where(filled[:, None, None], values, jnp.zeros_like(values))
-    wide = jnp.concatenate([kept, fresh_values], 0).transpose(1, 2, 0)
+    flat_values = values.reshape(cache_rows, kv_heads * width)
+    flat_values = jnp.where(filled[:, None], flat_values, jnp.zeros_like(flat_values))
+    flat_values = jnp.concatenate(
+        [flat_values, fresh_values.reshape(fresh_rows, kv_heads * width)], 0
+    )
+    flat_values = lax.optimization_barrier(flat_values)
+    wide = flat_values.T.reshape(kv_heads, width, cache_rows + fresh_rows)
     mask = jnp.concatenate([filled, jnp.ones((fresh_rows,), jnp.bool_)]).astype(jnp.bfloat16)
     mask = jnp.broadcast_to(mask[None, None, :], (kv_heads, 16, cache_rows + fresh_rows))
     wide = jnp.concatenate([wide, mask], 1).reshape(kv_heads * (width + 16), -1)
@@ -265,23 +270,33 @@
 
     step = rows // CHUNKS
     attended, mixed = [], []
+
+    def scatter(sums):
+        sums = lax.psum_scatter(sums, "tp", scatter_dimension=0, tiled=True)
+        return sums.reshape(ctx // tp, -1, sums.shape[-1])
+
     for c in range(CHUNKS):
         part = attention(
             queries, c * step, step, key_sets, value_sets, counts, low, position
         )
         attended.append(part)
         flat = part.reshape(step, heads * width)
-        halves = gather_pair(flat[: step // 2], flat[step // 2 :], ctx, c + 1)
-        everyone = jnp.concatenate(halves, 1).reshape(ctx * step, heads * width)
-        if mixed:
-            everyone, mixed[-1] = lax.optimization_barrier((everyone, mixed[-1]))
-        sums = jnp.dot(everyone, out_weight, preferred_element_type=jnp.float32)
-        sums = sums.astype(jnp.bfloat16)
-        queries, sums = lax.optimization_barrier((queries, sums))
-        sums = lax.psum_scatter(sums, "tp", scatter_dimension=0, tiled=True)
-        mixed.append(sums.reshape(ctx // tp, step, -1))
+        if c == 0:
+            pieces = [lax.all_gather(flat, "ctx", axis=0)]
+        else:
+            flat, partial = lax.optimization_barrier((flat, partial))
+            mixed.append(scatter(partial))
+            pieces = gather_pair(flat[: step // 2], flat[step // 2 :], ctx, c)
+        for index, piece in enumerate(pieces):
+            everyone = piece.reshape(-1, heads * width)
+            if index == 1:
+                mixed.append(scatter(partial))
+                everyone, mixed[-2] = lax.optimization_barrier((everyone, mixed[-2]))
+            partial = jnp.dot(everyone, out_weight, preferred_element_type=jnp.float32)
+            partial = partial.astype(jnp.bfloat16)
+    mixed.append(scatter(partial))
     attended = jnp.concatenate(attended, 0)
-    mixed = jnp.stack(mixed, 1).reshape(ctx // tp * rows, -1)
+    mixed = jnp.concatenate(mixed, 1).reshape(ctx // tp * rows, -1)
     return attended, mixed
 
 

time: 304 us -> 283 us (0.931); the launches traced: 300 us -> 283 us
  Pallas kernels: 168 us -> 151 us
  other arithmetic: 21.5 us -> 8.48 us
  waiting for transfers between devices: 42.9 us -> 53.6 us
  matrix products: 27.9 us -> 38.5 us
  local copies, waits for them, and re-layouts: 15.1 us -> 7.17 us
    pallas_call x3 -> x2, Pallas kernels: 102 us -> 80 us  [gather_pair(): pl.pallas_call(gather_kernel, out_shape=[jax.ShapeDtypeStruct((ctx,) + x....]
    reduce_scatter x2 -> x3, waiting for transfers between devices: 42.8 us -> 53.6 us  [scatter(): sums = lax.psum_scatter(sums, 'tp', scatter_dimension=0, tiled=True)]
    dot_general x2 -> x3, matrix products: 27.9 us -> 38.5 us  [on_device(): partial = jnp.dot(everyone, out_weight, preferred_element_type=jnp.float32)]
    concatenate x2 -> x1, other arithmetic: 7.38 us -> 2.09 us  [on_device(): mixed = jnp.concatenate(mixed, 1).reshape(ctx // tp * rows, -1)]
    pallas_call x2, Pallas kernels: 65.6 us -> 70.7 us  [attention(): pl.pallas_call(kernel, out_shape=jax.ShapeDtypeStruct((tokens, heads, wid...]
    select_n x2 -> x1, other arithmetic: 5.38 us -> 1.41 us  [pack(): jnp.where(filled[:, None], flat_values, jnp.zeros_like(flat_values))]
    broadcast_in_dim x1, local copies, waits for them, and re-layouts: 3.87 us -> 0.01 us  [pack(): jnp.broadcast_to(mask[None, None, :], (kv_heads, 16, cache_rows + fresh_r...]
  transfers between devices with their start and end apart: 2 -> 4, of which waited for: 1 -> 3; matrix products, arithmetic and copies ran while one was open for 3% -> 9% of each run, Pallas kernels for 19% -> 23%
where the time goes in v3:
time: 283 us
  Pallas kernels  151 us (53%)
  waiting for transfers between devices  53.6 us (19%)
  matrix products  38.5 us (14%)
  between operations  24.6 us (9%)
  other arithmetic  8.48 us (3%)
  local copies, waits for them, and re-layouts  7.17 us (3%)
    pallas_call x2, Pallas kernels, gather_pair(): pl.pallas_call(gather_kernel, out_shape=[jax.ShapeDtypeStruct((ctx,) + x....  80 us
    pallas_call x2, Pallas kernels, attention(): pl.pallas_call(kernel, out_shape=jax.ShapeDtypeStruct((tokens, heads, wid...  70.7 us
    reduce_scatter x3, waiting for transfers between devices, scatter(): sums = lax.psum_scatter(sums, 'tp', scatter_dimension=0, tiled=True)  53.6 us
    dot_general x3, matrix products, on_device(): partial = jnp.dot(everyone, out_weight, preferred_element_type=jnp.float32)  38.5 us
  transfers between devices with their start and end apart: 4, of which 3 were waited for; matrix products, arithmetic and copies ran while one was open for 9% of the time, Pallas kernels for 23%

profile of v3, /device:TPU:0, one launch (start us, length us, event | category | flops | bytes accessed | tf_op | source)
XLA Modules:
  0.0 283.3 jit_solution(17331530833408335434)
XLA Ops:
  7.2 0.6 fusion.2
  7.9 0.8 dynamic_slice.3
  8.6 0.9 convert_reduce_fusion
  9.5 0.6 fusion.1
  15.4 0.9 copy.27
  16.9 0.7 slice_bitcast_fusion.4
  17.6 0.8 copy.26
  18.4 1.4 bitcast_select_fusion
  19.8 0.9 pad_maximum_fusion.3
  20.7 0.3 copy.14
  21.0 0.9 pad_maximum_fusion.2
  21.9 50.2 %shard_map.95 = (bf16[8,1152,256]{2,1,0:T(8,128)(2,1)}, bf16[8,288,1152]{2,1,0:T(8,128)(2,1)}) custom-call(bf16[1152,256]{1,0:T(8,128)(2,1)} %get-tuple-element.30.a_ref, bf16[288,1152]{1,0:T(8,128)(2,1)} %bitcast.55), custom_call_target="tpu_custom_call" | custom-call | bytes 10027008 | tf_op jit(solution)/shard_map/pallas_call | solution.py:155
  72.1 1.1 convert_reduce_fusion.1
  73.4 0.1 reshape.91.lo_ref
  73.5 0.1 add_bitcast_fusion.bounds_ref
  73.6 35.3 %shard_map.96 = bf16[64,32,128]{2,1,0:T(8,128)(2,1)S(1)} custom-call(s32[8]{0:T(128)S(1)} %and_select_fusion.counts_ref, s32[2]{0:T(128)S(1)} %add_bitcast_fusion.bounds_ref, bf16[128,32,128]{2,1,0:T(8,128)(2,1)S(1)} %copy-done, s32[2,1024]{1,0:T(2,128)S(1)} %reshape.91.lo_ref, bf16[8,1152,256]{2,1,0:T(8,128)(2,1)} %get-tuple-element.11.k_ref, ...), custom_call_target="tpu_custom_call" | custom-call | flops 9663676416 | bytes 9437184 | tf_op jit(solution)/shard_map/pallas_call | solution.py:197
  108.9 1.0 all_gather_reshape.3
  114.8 0.1 broadcast_in_dim.50
  114.8 0.1 reshape.93.lo_ref
  115.0 35.3 %shard_map.97 = bf16[64,32,128]{2,1,0:T(8,128)(2,1)S(1)} custom-call(s32[8]{0:T(128)S(1)} %and_select_fusion.counts_ref, s32[2]{0:T(128)S(1)} %add_bitcast_fusion.1.bounds_ref, bf16[128,32,128]{2,1,0:T(8,128)(2,1)S(1)} %copy-done, s32[2,1024]{1,0:T(2,128)S(1)} %reshape.93.lo_ref, bf16[8,1152,256]{2,1,0:T(8,128)(2,1)} %get-tuple-element.11.k_ref, ...), custom_call_target="tpu_custom_call" | custom-call | flops 9663676416 | bytes 9437184 | tf_op jit(solution)/shard_map/pallas_call | solution.py:197
  150.4 0.2 copy.25
  150.6 14.6 %convolution_convert_fusion = bf16[512,2048]{1,0:T(8,128)(2,1)} fusion(bf16[512,4096]{1,0:T(8,128)(2,1)} %bitcast.69, bf16[4096,2048]{1,0:T(8,128)(2,1)} %param.15), kind=kOutput, calls=%fused_computation | convolution fusion | flops 8590983168 | bytes 23068672 | tf_op jit(solution)/shard_map/dot_general | solution.py:295
  165.3 0.8 fusion
  166.1 29.8 %shard_map.98 = (bf16[8,32,4096]{2,1,0:T(8,128)(2,1)}, bf16[8,32,4096]{2,1,0:T(8,128)(2,1)}) custom-call(bf16[32,4096]{1,0:T(8,128)(2,1)} %get-tuple-element.19.a_ref, bf16[32,4096]{1,0:T(8,128)(2,1)} %get-tuple-element.18.b_ref), custom_call_target="tpu_custom_call" | custom-call | bytes 4194304 | tf_op jit(solution)/shard_map/pallas_call | solution.py:155
  195.9 12.0 %convolution_convert_fusion.2 = bf16[256,2048]{1,0:T(8,128)(2,1)} fusion(bf16[256,4096]{1,0:T(8,128)(2,1)} %bitcast.71, bf16[4096,2048]{1,0:T(8,128)(2,1)} %param.15), kind=kOutput, calls=%fused_computation.2 | convolution fusion | flops 4295491584 | bytes 19922944 | tf_op jit(solution)/shard_map/dot_general | solution.py:295
  207.9 0.2 reduce-scatter.8.cloned.1.call-start
  208.1 9.1 %reduce-scatter.4.cloned.1.call-done = bf16[128,2048]{1,0:T(8,128)(2,1)} async-done(((bf16[512,2048]{1,0:T(8,128)(2,1)}), bf16[128,2048]{1,0:T(8,128)(2,1)}) %reduce-scatter.4.cloned.1.call-update) | async-done | bytes 524304 | tf_op jit(solution)/shard_map/reduce_scatter | solution.py:275
  217.2 11.9 %convolution_convert_fusion.1 = bf16[256,2048]{1,0:T(8,128)(2,1)} fusion(bf16[256,4096]{1,0:T(8,128)(2,1)} %bitcast.70, bf16[4096,2048]{1,0:T(8,128)(2,1)} %param.15), kind=kOutput, calls=%fused_computation.1 | convolution fusion | flops 4295491584 | bytes 19922944 | tf_op jit(solution)/shard_map/dot_general | solution.py:295
  229.1 1.1 pad_maximum_fusion
  230.2 15.9 %reduce-scatter.6.cloned.1.call-done = bf16[64,2048]{1,0:T(8,128)(2,1)} async-done(((bf16[256,2048]{1,0:T(8,128)(2,1)}), bf16[64,2048]{1,0:T(8,128)(2,1)}) %reduce-scatter.6.cloned.1.call-update) | async-done | bytes 262160 | tf_op jit(solution)/shard_map/reduce_scatter | solution.py:275
  246.1 28.6 %reduce-scatter.8.cloned.1.call-done = bf16[64,2048]{1,0:T(8,128)(2,1)} async-done(((bf16[256,2048]{1,0:T(8,128)(2,1)}), bf16[64,2048]{1,0:T(8,128)(2,1)}) %reduce-scatter.8.cloned.1.call-update) | async-done | bytes 262160 | tf_op jit(solution)/shard_map/reduce_scatter | solution.py:275
  274.7 2.1 pad_maximum_fusion.1
  (22 shorter events, 0.6 us)
Async XLA Ops:
  7.2 143.5 %all-gather.2.cloned.1.call-start = ((), (), s32[]{:S(2)}) async-start(), calls=%async_computation.3 | async-start | bytes 4718592 | tf_op jit(solution)/shard_map/all_gather | solution.py:285
  20.7 52.8 %copy-start = (bf16[128,32,128]{2,1,0:T(8,128)(2,1)S(1)}, bf16[128,32,128]{2,1,0:T(8,128)(2,1)}, u32[]{:S(2)}) copy-start(bf16[128,32,128]{2,1,0:T(8,128)(2,1)} %q_ref.3) | copy-start | bytes 3145732
  109.9 107.3 %reduce-scatter.4.cloned.1.call-start = ((), (), s32[]{:S(2)}) async-start(), calls=%async_computation.4 | async-start | bytes 2621440 | tf_op jit(solution)/shard_map/reduce_scatter | solution.py:275
  165.2 80.9 %reduce-scatter.6.cloned.1.call-start = ((), (), s32[]{:S(2)}) async-start(), calls=%async_computation.5 | async-start | bytes 1310720 | tf_op jit(solution)/shard_map/reduce_scatter | solution.py:275
  207.9 66.7 %reduce-scatter.8.cloned.1.call-start = ((), (), s32[]{:S(2)}) async-start(), calls=%async_computation.6 | async-start | bytes 1310720 | tf_op jit(solution)/shard_map/reduce_scatter | solution.py:275
  229.1 45.6 %copy-start.1 = (bf16[128,2048]{1,0:T(8,128)(2,1)S(1)}, bf16[128,2048]{1,0:T(8,128)(2,1)}, u32[]{:S(2)}) copy-start(bf16[128,2048]{1,0:T(8,128)(2,1)} %reduce-scatter.4.cloned.1.call-done) | copy-start | bytes 1572868
Sparse Core Ops, SparseCore 0:
  110.1 40.3 all-gather.1
  165.4 51.7 reduce-scatter.3
  219.6 26.4 reduce-scatter.5
  248.8 25.7 reduce-scatter.7
